TPU v7x, 32 devices: a whole 2x2x4 slice. The times are simulated.
32 devices in a mesh: harm: 4 (over z), node: 8 (over y, x, core).
Axes of the slice: x: 2, y: 2, z: 4, core: 2. Of those that a mesh axis runs over, the one named last changes fastest.
Arguments:
- adjoint: bfloat16 [128, 4, 32768], P('harm', None, 'node'), may hold values from -6 to 6
- source: float32 [128, 131072], P(None, ('harm', 'node')), may hold values from -6 to 6
- rad_coeff: bfloat16 [128, 131072], P(None, ('harm', 'node')), may hold values from 0.19921875 to 2
- capacity: float32 [131072], P(('harm', 'node')), may hold values from 0.005 to 0.03
- inv_diag: float32 [131072], P(('harm', 'node')), may hold values from 0.1 to 0.5
- blocks: bfloat16 [1024, 4, 128, 128], P(('harm', 'node')), may hold values from -0.25 to 0.25
- block_cols: int32 [1024, 4], P(('harm', 'node')), may hold values from 0 to 1023, as said below
- zone_of: int32 [131072], P(('harm', 'node')), may hold values from 0 to 1279, as said below
- heater_weight: float32 [131072], P(('harm', 'node')), may hold values from 0.2 to 2
Outputs:
- updated: bfloat16 [128, 4, 32768], P('harm', None, 'node')
- gradient: float32 [1280, 128], P(('harm', 'node'))
Inputs may be any that keep to these rules, and one draw needn't show every extreme that they name: `block_cols`: with d = b // 32 and D = 32: slot 0 of row block b names b itself; slot 1 lies in row blocks max(d - 1, 0) * 32 to (max(d - 1, 0) + 1) * 32 - 1; slot 2 in min(d + 1, D - 1) * 32 to (min(d + 1, D - 1) + 1) * 32 - 1; the other slots in (d - 1) * 32 to (d + 2) * 32 - 1. `zone_of`: node n lies in a zone z with (n // 4096 - 1) * 40 <= z < (n // 4096 + 2) * 40.
All inputs are finite; a program needn't handle non-finite values.
Results may differ from a plain program's by a relative error of at most 0.0035.
Values may be sent and summed in bfloat16 or wider, within the bound.
A program may use at most 64 MiB of HBM per device.

v0:
```python
import math

import jax
import jax.numpy as jnp
from jax import lax
from jax.sharding import PartitionSpec as P

ZONE_DEV = 40


def with_halo(value, sides, width):
    for axis, dim in sides:
        count, length = (lax.axis_size(axis), value.shape[dim])
        up = [(i, (i + 1) % count) for i in range(count - 1)]
        down = [(j, i) for i, j in up]
        last = lax.slice_in_dim(value, length - width, length, axis=dim)
        initial = lax.slice_in_dim(value, 0, width, axis=dim)
        before = lax.ppermute(last, axis, up)
        after = lax.ppermute(initial, axis, down)
        value = jnp.concatenate([before, value, after], axis=dim)
    return value


def passed_along(value, axis, steps):
    count = lax.axis_size(axis)
    initial, last = (max(0, -steps), min(count, count - steps))
    return lax.ppermute(value, axis, [(source, source + steps) for source in range(initial, last)])


def fourier_basis(count):
    sample_index = jnp.arange(count, dtype=jnp.float32)[:, None]
    column_index = jnp.arange(count)[None, :]
    half_count = count // 2
    frequency = jnp.where(
        column_index <= half_count, column_index, column_index - half_count
    ).astype(jnp.float32)
    angle = 2.0 * math.pi * frequency * sample_index / count
    values_table = jnp.where(column_index <= half_count, jnp.cos(angle), jnp.sin(angle))
    scaling = jnp.where(
        (column_index == 0) | (column_index == half_count),
        math.sqrt(1.0 / count),
        math.sqrt(2.0 / count),
    )
    return (values_table * scaling).astype(jnp.bfloat16)


def derivative_term(field):
    half_count = field.shape[0] // 2
    wave_number = jnp.arange(1, half_count, dtype=jnp.float32)[:, None]
    zero_row = jnp.zeros((1, field.shape[1]), jnp.float32)
    upper_rows = wave_number * field[half_count + 1 :]
    lower_rows = -wave_number * field[1:half_count]
    return jnp.concatenate([zero_row, upper_rows, zero_row, lower_rows], axis=0)


def body(
    adjoint, source, rad_coeff, capacity, inv_diag, blocks, block_cols, zone_of, heater_weight
):
    arrived = lax.all_to_all(adjoint, "harm", split_axis=1, concat_axis=0, tiled=True)
    harmonics = arrived.shape[0]
    node_count = arrived.shape[2]
    field = arrived.reshape(harmonics, node_count)
    block_size = blocks.shape[2]
    row_blocks = node_count // block_size
    fourier = fourier_basis(harmonics)
    samples = jnp.dot(fourier, field, preferred_element_type=jnp.float32)
    weighted = (rad_coeff.astype(jnp.float32) * samples).astype(jnp.bfloat16)
    radiative = jnp.dot(fourier.T, weighted, preferred_element_type=jnp.float32)
    rate_term = derivative_term(field.astype(jnp.float32))
    padded = with_halo(field, ((("harm", "node"), 1),), node_count)
    position = lax.axis_index(("harm", "node"))
    local_cols = block_cols - (position - 1) * row_blocks
    extended = padded.reshape(harmonics, 3 * row_blocks, block_size)
    gathered = jnp.take(extended, local_cols, axis=1)
    conduction = jnp.einsum(
        "kbsj,bsij->kbi", gathered, blocks, preferred_element_type=jnp.float32
    ).reshape(harmonics, node_count)
    residual = source - (capacity[None, :] * rate_term + conduction + radiative)
    updated = (field.astype(jnp.float32) + inv_diag[None, :] * residual).astype(jnp.bfloat16)
    returned = lax.all_to_all(
        updated.reshape(harmonics, 1, node_count), "harm", split_axis=0, concat_axis=1, tiled=True
    )
    weighted_terms = (updated.astype(jnp.float32) * heater_weight[None, :]).T
    window_zone = zone_of - (position - 1) * ZONE_DEV
    selector = (window_zone[:, None] == jnp.arange(3 * ZONE_DEV, dtype=jnp.int32)[None, :]).astype(
        jnp.float32
    )
    window_sums = jnp.einsum("nz,nk->zk", selector, weighted_terms, precision=lax.Precision.HIGHEST)
    lower_part = window_sums[:ZONE_DEV]
    middle_part = window_sums[ZONE_DEV : 2 * ZONE_DEV]
    upper_part = window_sums[2 * ZONE_DEV :]
    above_terms = passed_along(lower_part, ("harm", "node"), -1)
    below_terms = passed_along(upper_part, ("harm", "node"), 1)
    gradient = middle_part + above_terms + below_terms
    return (returned, gradient)


def solution(mesh):
    in_specs = (
        P("harm", None, "node"),
        P(None, ("harm", "node")),
        P(None, ("harm", "node")),
        P(("harm", "node")),
        P(("harm", "node")),
        P(("harm", "node"), None, None, None),
        P(("harm", "node"), None),
        P(("harm", "node")),
        P(("harm", "node")),
    )
    out_specs = (P("harm", None, "node"), P(("harm", "node"), None))
    return jax.shard_map(body, mesh=mesh, in_specs=in_specs, out_specs=out_specs, check_vma=False)
```

profile of v0, /device:TPU:4, one launch (start us, length us, event | category | flops | bytes accessed | tf_op | source)
XLA Modules:
  0.0 116.6 jit_solution(15993468261064862405)
XLA Ops:
  0.6 0.0 copy-start.6
  0.6 2.8 %copy.35 = bf16[32,4,4096]{2,0,1:T(8,128)(2,1)} copy(bf16[32,4,4096]{2,1,0:T(4,128)(2,1)} %param.9) | data formatting | bytes 2097152 | tf_op args[0]
  3.4 4.9 %all-to-all-start = ((bf16[32,4,4096]{2,0,1:T(8,128)(2,1)}), bf16[32,4,4096]{2,0,1:T(8,128)(2,1)S(1)}, u32[]{:S(2)}, u32[]{:S(2)}) async-start(bf16[32,4,4096]{2,0,1:T(8,128)(2,1)} %copy.35), calls=%async_computation | async-start | bytes 2097152 | tf_op jit(solution)/shard_map/all_to_all | solution.py:59
  8.3 0.0 copy-done.6
  8.3 0.1 copy.40
  8.4 0.1 reshape.72
  8.5 0.1 copy.36
  8.6 25.4 %all-to-all-done = bf16[32,4,4096]{2,0,1:T(8,128)(2,1)S(1)} async-done(((bf16[32,4,4096]{2,0,1:T(8,128)(2,1)}), bf16[32,4,4096]{2,0,1:T(8,128)(2,1)S(1)}, u32[]{:S(2)}, u32[]{:S(2)}) %all-to-all-start) | async-done | bytes 1048608 | tf_op jit(solution)/shard_map/all_to_all | solution.py:59
  34.0 0.0 copy-start
  34.0 2.0 %collective-permute-start.1 = (bf16[128,4096]{1,0:T(8,128)(2,1)S(1)}, bf16[128,4096]{1,0:T(8,128)(2,1)S(1)}, u32[]{:S(2)}, u32[]{:S(2)}) collective-permute-start(bf16[128,4096]{1,0:T(8,128)(2,1)S(1)} %bitcast.39), channel_id=1, source_target_pairs={{1,0},{2,1},{3,2},{4,3},{5,4},{6,5},{7,6},{8,7},{9,8},{10,9},{11,1... | collective-permute-start | bytes 3145736 | tf_op jit(solution)/shard_map/ppermute | solution.py:19
  36.0 2.3 %collective-permute-start = (bf16[128,4096]{1,0:T(8,128)(2,1)S(1)}, bf16[128,4096]{1,0:T(8,128)(2,1)S(1)}, u32[]{:S(2)}, u32[]{:S(2)}) collective-permute-start(bf16[128,4096]{1,0:T(8,128)(2,1)S(1)} %bitcast.40), channel_id=1, source_target_pairs={{0,1},{1,2},{2,3},{3,4},{4,5},{5,6},{6,7},{7,8},{8,9},{9,10},{10,1... | collective-permute-start | bytes 3145736 | tf_op jit(solution)/shard_map/ppermute | solution.py:18
  38.3 0.3 bitcast_convert_fusion
  38.6 0.2 copy.48
  38.9 0.0 copy-done
  38.9 0.4 copy.38
  39.3 1.6 %slice_multiply_fusion.1 = (f32[63,4096]{1,0:T(8,128)}, f32[63,4096]{1,0:T(8,128)}) fusion(f32[128,4096]{1,0:T(8,128)S(1)} %bitcast_convert_fusion, f32[63]{0:T(128)S(1)} %get-tuple-element.10, f32[63]{0:T(128)S(1)} %get-tuple-element.11), kind=kLoop, calls=%fused_computation.24 | loop fusion | flops 516096 | bytes 4129272 | tf_op jit(solution)/shard_map/mul | solution.py:51
  40.9 15.8 %collective-permute-done.1 = bf16[128,4096]{1,0:T(8,128)(2,1)S(1)} collective-permute-done((bf16[128,4096]{1,0:T(8,128)(2,1)S(1)}, bf16[128,4096]{1,0:T(8,128)(2,1)S(1)}, u32[]{:S(2)}, u32[]{:S(2)}) %collective-permute-start.1) | collective-permute-done | bytes 1048608 | tf_op jit(solution)/shard_map/ppermute | solution.py:19
  56.7 0.3 copy_bitcast_fusion
  57.0 4.3 %collective-permute-done = bf16[128,4096]{1,0:T(8,128)(2,1)S(1)} collective-permute-done((bf16[128,4096]{1,0:T(8,128)(2,1)S(1)}, bf16[128,4096]{1,0:T(8,128)(2,1)S(1)}, u32[]{:S(2)}, u32[]{:S(2)}) %collective-permute-start) | collective-permute-done | bytes 1048608 | tf_op jit(solution)/shard_map/ppermute | solution.py:18
  61.4 0.3 copy_bitcast_fusion.1
  61.6 0.4 pad_maximum_fusion
  62.0 3.0 %gather_fusion = bf16[128,128,128]{2,1,0:T(8,128)(2,1)} fusion(bf16[128,96,128]{2,0,1:T(8,128)(2,1)S(1)} %pad_maximum_fusion, s32[1024]{0:T(1024)S(1)} %pad_clamp_fusion), kind=kCustom, calls=%fused_computation | custom fusion | bytes 8389120 | tf_op jit(solution)/shard_map/jit(_take)/gather | solution.py:74
  65.1 6.2 %fusion.5 = f32[32,128,128,1]{1,2,3,0:T(8,128)} fusion(bf16[32,4,128,128]{3,2,1,0:T(8,128)(2,1)} %param.14, bf16[32,4,128,128]{3,2,1,0:T(8,128)(2,1)} %bitcast.44, pred[32,4]{1,0:T(8,128)(4,1)S(1)} %copy.36), kind=kOutput, calls=%fused_computation.8 | convolution fusion | flops 538968064 | bytes 10485888 | tf_op jit(solution)/shard_map/kbsj,bsij->kbi/dot_general | solution.py:75
  71.3 2.0 %copy.41 = f32[128,4096]{1,0:T(8,128)S(1)} copy(f32[128,4096]{0,1:T(8,128)} %bitcast.47) | data formatting | bytes 4194304 | tf_op jit(solution)/shard_map/reshape | solution.py:77
  73.3 0.0 copy-done.1
  73.3 0.0 copy-done.3
  73.3 0.0 copy-done.4
  73.3 5.2 %fusion.4 = bf16[128,4096]{1,0:T(8,128)(2,1)} fusion(f32[128,4096]{1,0:T(8,128)} %param.10, f32[128,4096]{1,0:T(8,128)S(1)} %copy.41, f32[63,4096]{1,0:T(8,128)} %get-tuple-element.7, f32[1,4096]{1,0:T(1,128)S(1)} %broadcast_in_dim.41, f32[63,4096]{1,0:T(8,128)} %get-tuple-element.6, bf16[128,4096]{1,0:T(8,128)(2,1)S(1)} %bitcast.42, ...), kind=kOutput, calls=%fused_computation.7 | convolution fusion | flops 275939328 | bytes 9454720 | tf_op jit(solution)/shard_map/dot_general | solution.py:68
  78.5 0.5 broadcast.81
  79.0 2.6 %reduce = bf16[128,4096]{1,0:T(8,128)(2,1)S(1)} reduce(bf16[128,1,4096]{2,0,1:T(8,128)(2,1)} %bitcast.46, bf16[]{:T(256)} %broadcast.81), dimensions={1}, to_apply=%copy.42.reduce_sub_computation | reduce | bytes 2097154 | tf_op jit(solution)/shard_map/reshape | solution.py:81
  81.7 0.0 copy-start.5
  81.7 0.0 copy-start.2
  81.7 0.0 copy-start.7
  81.7 2.0 %reshape.81 = bf16[4,2,65536]{2,1,0:T(2,128)(2,1)} reshape(bf16[128,4096]{1,0:T(8,128)(2,1)S(1)} %reduce) | data formatting | bytes 2097152
  83.7 3.5 %all-to-all-start.1 = ((bf16[4,2,65536]{2,1,0:T(2,128)(2,1)}), bf16[4,2,65536]{2,1,0:T(2,128)(2,1)S(1)}, u32[]{:S(2)}, u32[]{:S(2)}) async-start(bf16[4,2,65536]{2,1,0:T(2,128)(2,1)} %reshape.81), calls=%async_computation.1 | async-start | bytes 2097152 | tf_op jit(solution)/shard_map/all_to_all | solution.py:80
  87.2 0.0 copy-done.5
  87.2 0.0 copy-done.2
  87.3 0.0 copy-done.7
  87.3 2.1 %fusion.11 = f32[120,128]{1,0:T(8,128)S(1)} fusion(bf16[128,4096]{1,0:T(8,128)(2,1)S(1)} %copy-done.2, f32[4096]{0:T(1024)S(1)} %copy-done.7, s32[4096]{0:T(1024)S(1)} %broadcast_subtract_fusion), kind=kOutput, calls=%fused_computation.16 | convolution fusion | flops 757006336 | bytes 1142784 | tf_op jit(solution)/shard_map/nz,nk->zk/dot_general | solution.py:88
  89.4 1.9 %collective-permute-start.2 = (f32[40,128]{1,0:T(8,128)S(1)}, f32[40,128]{1,0:T(8,128)S(1)}, u32[]{:S(2)}, u32[]{:S(2)}) collective-permute-start(f32[40,128]{1,0:T(8,128)S(1)} %get-tuple-element.8), channel_id=1, source_target_pairs={{1,0},{2,1},{3,2},{4,3},{5,4},{6,5},{7,6},{8,7},{9,8},{10,9},{11,1... | collective-permute-start | bytes 61448 | tf_op jit(solution)/shard_map/ppermute | solution.py:27
  91.3 2.4 %collective-permute-start.3 = (f32[40,128]{1,0:T(8,128)S(1)}, f32[40,128]{1,0:T(8,128)S(1)}, u32[]{:S(2)}, u32[]{:S(2)}) collective-permute-start(f32[40,128]{1,0:T(8,128)S(1)} %get-tuple-element.9), channel_id=1, source_target_pairs={{0,1},{1,2},{2,3},{3,4},{4,5},{5,6},{6,7},{7,8},{8,9},{9,10},{10,1... | collective-permute-start | bytes 61448 | tf_op jit(solution)/shard_map/ppermute | solution.py:27
  93.7 0.0 collective-permute-done.2
  93.7 3.6 %collective-permute-done.3 = f32[40,128]{1,0:T(8,128)S(1)} collective-permute-done((f32[40,128]{1,0:T(8,128)S(1)}, f32[40,128]{1,0:T(8,128)S(1)}, u32[]{:S(2)}, u32[]{:S(2)}) %collective-permute-start.3) | collective-permute-done | bytes 20512 | tf_op jit(solution)/shard_map/ppermute | solution.py:27
  97.3 0.6 fusion.26
  97.9 14.8 %all-to-all-done.1 = bf16[4,2,65536]{2,1,0:T(2,128)(2,1)S(1)} async-done(((bf16[4,2,65536]{2,1,0:T(2,128)(2,1)}), bf16[4,2,65536]{2,1,0:T(2,128)(2,1)S(1)}, u32[]{:S(2)}, u32[]{:S(2)}) %all-to-all-start.1) | async-done | bytes 1048608 | tf_op jit(solution)/shard_map/all_to_all | solution.py:80
  112.7 0.9 reshape.82
  113.7 1.1 copy.45
  114.9 1.8 %copy.43 = bf16[32,4,4096]{2,1,0:T(4,128)(2,1)} copy(bf16[32,4,4096]{2,0,1:T(8,128)(2,1)S(1)} %bitcast.43) | data formatting | bytes 2097152
  (11 shorter events, 0.1 us)
Async XLA Ops:
  0.6 7.7 %copy-start.6 = (s32[32,4]{0,1:T(4,128)S(1)}, s32[32,4]{0,1:T(4,128)}, u32[]{:S(2)}) copy-start(s32[32,4]{0,1:T(4,128)} %param.15) | copy-start | bytes 1540
  3.4 30.6 %all-to-all-start = ((bf16[32,4,4096]{2,0,1:T(8,128)(2,1)}), bf16[32,4,4096]{2,0,1:T(8,128)(2,1)S(1)}, u32[]{:S(2)}, u32[]{:S(2)}) async-start(bf16[32,4,4096]{2,0,1:T(8,128)(2,1)} %copy.35), calls=%async_computation | async-start | bytes 2097152 | tf_op jit(solution)/shard_map/all_to_all | solution.py:59
  34.0 4.9 %copy-start = (bf16[32,4,4096]{2,0,1:T(8,128)(2,1)}, bf16[32,4,4096]{2,0,1:T(8,128)(2,1)S(1)}, u32[]{:S(2)}) copy-start(bf16[32,4,4096]{2,0,1:T(8,128)(2,1)S(1)} %all-to-all-done) | copy-start | bytes 3145732
  34.0 22.7 %collective-permute-start.1 = (bf16[128,4096]{1,0:T(8,128)(2,1)S(1)}, bf16[128,4096]{1,0:T(8,128)(2,1)S(1)}, u32[]{:S(2)}, u32[]{:S(2)}) collective-permute-start(bf16[128,4096]{1,0:T(8,128)(2,1)S(1)} %bitcast.39), channel_id=1, source_target_pairs={{1,0},{2,1},{3,2},{4,3},{5,4},{6,5},{7,6},{8,7},{9,8},{10,9},{11,1... | collective-permute-start | bytes 3145736 | tf_op jit(solution)/shard_map/ppermute | solution.py:19
  36.0 25.3 %collective-permute-start = (bf16[128,4096]{1,0:T(8,128)(2,1)S(1)}, bf16[128,4096]{1,0:T(8,128)(2,1)S(1)}, u32[]{:S(2)}, u32[]{:S(2)}) collective-permute-start(bf16[128,4096]{1,0:T(8,128)(2,1)S(1)} %bitcast.40), channel_id=1, source_target_pairs={{0,1},{1,2},{2,3},{3,4},{4,5},{5,6},{6,7},{7,8},{8,9},{9,10},{10,1... | collective-permute-start | bytes 3145736 | tf_op jit(solution)/shard_map/ppermute | solution.py:18
  71.3 2.0 %copy-start.1 = (bf16[32,4,4096]{2,0,1:T(8,128)(2,1)S(1)}, bf16[32,4,4096]{2,0,1:T(8,128)(2,1)}, u32[]{:S(2)}) copy-start(bf16[32,4,4096]{2,0,1:T(8,128)(2,1)} %copy-done) | copy-start | bytes 3145732
  71.3 2.0 %copy-start.3 = (f32[4096]{0:T(1024)S(1)}, f32[4096]{0:T(1024)}, u32[]{:S(2)}) copy-start(f32[4096]{0:T(1024)} %param.12) | copy-start | bytes 49156
  71.3 2.1 %copy-start.4 = (f32[4096]{0:T(1024)S(1)}, f32[4096]{0:T(1024)}, u32[]{:S(2)}) copy-start(f32[4096]{0:T(1024)} %param.13) | copy-start | bytes 49156
  81.7 5.6 %copy-start.5 = (s32[4096]{0:T(1024)S(1)}, s32[4096]{0:T(1024)}, u32[]{:S(2)}) copy-start(s32[4096]{0:T(1024)} %param.16) | copy-start | bytes 49156
  81.7 5.6 %copy-start.2 = (bf16[128,4096]{1,0:T(8,128)(2,1)S(1)}, bf16[128,4096]{1,0:T(8,128)(2,1)}, u32[]{:S(2)}) copy-start(bf16[128,4096]{1,0:T(8,128)(2,1)} %fusion.4) | copy-start | bytes 3145732
  81.7 5.6 %copy-start.7 = (f32[4096]{0:T(1024)S(1)}, f32[4096]{0:T(1024)}, u32[]{:S(2)}) copy-start(f32[4096]{0:T(1024)} %param.17) | copy-start | bytes 49156
  83.7 29.0 %all-to-all-start.1 = ((bf16[4,2,65536]{2,1,0:T(2,128)(2,1)}), bf16[4,2,65536]{2,1,0:T(2,128)(2,1)S(1)}, u32[]{:S(2)}, u32[]{:S(2)}) async-start(bf16[4,2,65536]{2,1,0:T(2,128)(2,1)} %reshape.81), calls=%async_computation.1 | async-start | bytes 2097152 | tf_op jit(solution)/shard_map/all_to_all | solution.py:80
  89.4 4.3 %collective-permute-start.2 = (f32[40,128]{1,0:T(8,128)S(1)}, f32[40,128]{1,0:T(8,128)S(1)}, u32[]{:S(2)}, u32[]{:S(2)}) collective-permute-start(f32[40,128]{1,0:T(8,128)S(1)} %get-tuple-element.8), channel_id=1, source_target_pairs={{1,0},{2,1},{3,2},{4,3},{5,4},{6,5},{7,6},{8,7},{9,8},{10,9},{11,1... | collective-permute-start | bytes 61448 | tf_op jit(solution)/shard_map/ppermute | solution.py:27
  91.3 6.0 %collective-permute-start.3 = (f32[40,128]{1,0:T(8,128)S(1)}, f32[40,128]{1,0:T(8,128)S(1)}, u32[]{:S(2)}, u32[]{:S(2)}) collective-permute-start(f32[40,128]{1,0:T(8,128)S(1)} %get-tuple-element.9), channel_id=1, source_target_pairs={{0,1},{1,2},{2,3},{3,4},{4,5},{5,6},{6,7},{7,8},{8,9},{9,10},{10,1... | collective-permute-start | bytes 61448 | tf_op jit(solution)/shard_map/ppermute | solution.py:27
where the time goes:
time: 117 us
  waiting for transfers between devices  63.9 us (55%)
  starting transfers between devices  17 us (15%)
  local copies, waits for them, and re-layouts  15.8 us (14%)
  matrix products  13.5 us (12%)
  other arithmetic  5.56 us (5%)
    all_to_all x1, waiting for transfers between devices, body(): lax.all_to_all(adjoint, 'harm', split_axis=1, concat_axis=0, tiled=True)  25.4 us
    ppermute x1, waiting for transfers between devices, with_halo(): after = lax.ppermute(initial, axis, down)  15.8 us
    all_to_all x1, waiting for transfers between devices, body(): lax.all_to_all(updated.reshape(harmonics, 1, node_count), 'harm', split_a...  14.8 us
    unnamed x22, local copies, waits for them, and re-layouts  8.93 us
    dot_general x1, matrix products, body(): jnp.einsum('kbsj,bsij->kbi', gathered, blocks, preferred_element_type=jnp...  6.17 us
    dot_general x1, matrix products, body(): radiative = jnp.dot(fourier.T, weighted, preferred_element_type=jnp.float32)  5.2 us
    all_to_all x1, starting transfers between devices, body(): lax.all_to_all(adjoint, 'harm', split_axis=1, concat_axis=0, tiled=True)  4.87 us
    ppermute x2, starting transfers between devices, passed_along(): lax.ppermute(value, axis, [(source, source + steps) for source in range(i...  4.33 us
  transfers between devices with their start and end apart: 6, of which 5 were waited for; matrix products, arithmetic and copies ran while one was open for 5% of the time, Pallas kernels for 0%

commit v1 on v0

v1 whole, which is shorter than its diff:
```python
import functools
import math

import jax
import jax.numpy as jnp
import numpy as np
from jax import lax
from jax.experimental import pallas as pl
from jax.experimental.pallas import tpu as pltpu
from jax.sharding import PartitionSpec as P

ZONE_DEV = 40
ROWS = 16
GROUPS = 4
WIDTH = 256
MESH = pl.DeviceIdType.MESH
NT = (((1,), (1,)), ((), ()))


def fourier_basis(count):
    sample_index = np.arange(count, dtype=np.float32)[:, None]
    column_index = np.arange(count)[None, :]
    half_count = count // 2
    frequency = np.where(
        column_index <= half_count, column_index, column_index - half_count
    ).astype(np.float32)
    angle = np.float32(2.0 * math.pi) * frequency * sample_index / np.float32(count)
    values_table = np.where(column_index <= half_count, np.cos(angle), np.sin(angle))
    scaling = np.where(
        (column_index == 0) | (column_index == half_count),
        math.sqrt(1.0 / count),
        math.sqrt(2.0 / count),
    ).astype(np.float32)
    return (values_table * scaling).astype(jnp.bfloat16)


def kernel(
    n_harm,
    n_node,
    n_chunk,
    adj,
    src_any,
    rad_any,
    blk_any,
    capacity,
    inv_diag,
    weight,
    zone,
    cols,
    fourier,
    fourier_t,
    rate_k,
    ret,
    grad,
    *scratch,
):
    ext = scratch[:n_chunk]
    (
        src,
        rad,
        blk,
        upd,
        select,
        part,
        from_prev,
        from_next,
        load_sem,
        in_send,
        in_recv,
        halo_send,
        halo_recv,
        out_send,
        out_recv,
        own_sem,
        part_send,
        part_recv,
    ) = scratch[n_chunk:]
    row_blocks = adj.shape[2]
    nodes = row_blocks * 128
    chunk_rows = n_harm * ROWS
    me_h = lax.axis_index("harm")
    me_n = lax.axis_index("node")
    pos = me_h * n_node + me_n
    last = n_harm * n_node - 1
    has_prev = pos > 0
    has_next = pos < last
    prev = jnp.maximum(pos - 1, 0)
    following = jnp.minimum(pos + 1, last)
    prev_id = (prev // n_node, prev % n_node)
    next_id = (following // n_node, following % n_node)
    sides = ((has_prev, prev_id, 2), (has_next, next_id, 0))

    loads = [
        pltpu.make_async_copy(src_any, src, load_sem.at[0]),
        pltpu.make_async_copy(rad_any, rad, load_sem.at[1]),
        pltpu.make_async_copy(blk_any, blk, load_sem.at[2]),
    ]
    own = [
        pltpu.make_async_copy(
            adj.at[me_h, c], ext[c].at[me_h, pl.ds(row_blocks, row_blocks)], load_sem.at[3 + c]
        )
        for c in range(n_chunk)
    ]

    barrier = pltpu.get_barrier_semaphore()
    for d in range(1, n_harm):
        peer = lax.rem(me_h + d, n_harm)
        pl.semaphore_signal(barrier, inc=1, device_id=(peer, me_n), device_id_type=MESH)
    for there, device, _ in sides:

        @pl.when(there)
        def _(device=device):
            pl.semaphore_signal(barrier, inc=1, device_id=device, device_id_type=MESH)

    pl.semaphore_wait(
        barrier, n_harm - 1 + has_prev.astype(jnp.int32) + has_next.astype(jnp.int32)
    )

    def arrive(d, c):
        peer = lax.rem(me_h + d, n_harm)
        return pltpu.make_async_remote_copy(
            src_ref=adj.at[peer, c],
            dst_ref=ext[c].at[me_h, pl.ds(row_blocks, row_blocks)],
            send_sem=in_send.at[d, c],
            recv_sem=in_recv.at[d, c],
            device_id=(peer, me_n),
            device_id_type=MESH,
        )

    def halo(d, c, side):
        _, device, place = sides[side]
        piece = lax.rem(me_h - d + n_harm, n_harm)
        if d == 0:
            source = adj.at[me_h, c]
        else:
            source = ext[c].at[piece, pl.ds(row_blocks, row_blocks)]
        return pltpu.make_async_remote_copy(
            src_ref=source,
            dst_ref=ext[c].at[piece, pl.ds(place * row_blocks, row_blocks)],
            send_sem=halo_send.at[side, d, c],
            recv_sem=halo_recv.at[side, d, c],
            device_id=device,
            device_id_type=MESH,
        )

    def start_halo(d, c):
        for side in range(2):

            @pl.when(sides[side][0])
            def _(side=side):
                halo(d, c, side).start()

    for c in range(n_chunk):
        for d in range(1, n_harm):
            arrive(d, c).start()
        own[c].start()
        start_halo(0, c)
    for load in loads:
        load.start()

    zone_row = lax.broadcasted_iota(jnp.int32, (128, WIDTH), 0)

    def select_step(i, carry):
        at = pl.ds(pl.multiple_of(i * WIDTH, WIDTH), WIDTH)
        hit = zone_row == (zone[:, at] - (pos - 1) * ZONE_DEV)
        w = weight[:, at]
        high = w.astype(jnp.bfloat16).astype(jnp.float32)
        select[0:128, at] = jnp.where(hit, high, 0.0).astype(jnp.bfloat16)
        select[128:256, at] = jnp.where(hit, w - high, 0.0).astype(jnp.bfloat16)
        return carry

    lax.fori_loop(0, nodes // WIDTH, select_step, 0)

    for c in range(n_chunk):
        own[c].wait()
        for d in range(1, n_harm):
            arrive(d, c).wait_recv()
            start_halo(d, c)
    for load in loads:
        load.wait()

    def block_of(c, index):
        return jnp.concatenate([ext[c][h, index] for h in range(n_harm)], axis=0)

    half = chunk_rows // 2

    def local_step(i, carry):
        at = pl.ds(pl.multiple_of(i * WIDTH, WIDTH), WIDTH)
        first = row_blocks + i * (WIDTH // 128)
        pieces = [
            jnp.concatenate([block_of(c, first + t) for t in range(WIDTH // 128)], axis=1)
            for c in range(n_chunk)
        ]
        field = jnp.concatenate(pieces, axis=0) if n_chunk > 1 else pieces[0]
        samples = jnp.dot(fourier[...], field, preferred_element_type=jnp.float32)
        weighted = (rad[:, at].astype(jnp.float32) * samples).astype(jnp.bfloat16)
        radiative = jnp.dot(fourier_t[...], weighted, preferred_element_type=jnp.float32)
        cap = capacity[:, at]
        for c in range(n_chunk):
            lam = pieces[c].astype(jnp.float32)
            swapped = jnp.concatenate([lam[half:], lam[:half]], axis=0)
            rows = slice(c * chunk_rows, (c + 1) * chunk_rows)
            rate = rate_k[rows, :] * swapped
            rest = src[:, c, :, at].reshape(chunk_rows, WIDTH) - (cap * rate + radiative[rows])
            src[:, c, :, at] = rest.reshape(n_harm, ROWS, WIDTH)
        return carry

    lax.fori_loop(0, nodes // WIDTH, local_step, 0)

    group = nodes // GROUPS
    group_blocks = group // 128

    def back(d, c, q):
        peer = lax.rem(me_h + d, n_harm)
        return pltpu.make_async_remote_copy(
            src_ref=upd.at[peer, c, :, pl.ds(q * group, group)],
            dst_ref=ret.at[me_h, c, :, pl.ds(q * group, group)],
            send_sem=out_send.at[d, c, q],
            recv_sem=out_recv.at[d, c, q],
            device_id=(peer, me_n),
            device_id_type=MESH,
        )

    def own_back(c, q):
        return pltpu.make_async_copy(
            upd.at[me_h, c, :, pl.ds(q * group, group)],
            ret.at[me_h, c, :, pl.ds(q * group, group)],
            own_sem.at[c, q],
        )

    for c in range(n_chunk):
        for side in range(2):

            @pl.when(sides[1 - side][0])
            def _(side=side, c=c):
                for d in range(n_harm):
                    halo(d, c, side).wait_recv()

        for q in range(GROUPS):

            def block_step(i, carry, c=c, q=q):
                b = q * group_blocks + i
                at = pl.ds(pl.multiple_of(b * 128, 128), 128)
                lam = block_of(c, row_blocks + b)
                taken = [lam]
                for s in range(1, blk.shape[1]):
                    col = cols[s, b] - (pos - 1) * row_blocks
                    col = jnp.minimum(jnp.maximum(col, 0), 3 * row_blocks - 1)
                    taken.append(block_of(c, col))
                conductance = jnp.concatenate(
                    [blk[b, s] for s in range(blk.shape[1])], axis=1
                )
                conduction = lax.dot_general(
                    jnp.concatenate(taken, axis=1),
                    conductance,
                    NT,
                    preferred_element_type=jnp.float32,
                )
                residual = src[:, c, :, at].reshape(chunk_rows, 128) - conduction
                new = lam.astype(jnp.float32) + inv_diag[:, at] * residual
                upd[:, c, :, at] = new.astype(jnp.bfloat16).reshape(n_harm, ROWS, 128)
                return carry

            lax.fori_loop(0, group_blocks, block_step, 0, unroll=2)
            for d in range(1, n_harm):
                back(d, c, q).start()
            own_back(c, q).start()

    part[...] = jnp.zeros_like(part)

    def gradient_step(i, carry):
        at = pl.ds(pl.multiple_of(i * 512, 512), 512)
        new = upd[:, :, :, at].reshape(n_chunk * chunk_rows, 512)
        both = lax.dot_general(select[:, at], new, NT, preferred_element_type=jnp.float32)
        part[...] += both[0:128] + both[128:256]
        return carry

    lax.fori_loop(0, nodes // 512, gradient_step, 0)

    def hand_over(side):
        _, device, place = sides[side]
        rows = pl.ds(0 if side == 0 else 2 * ZONE_DEV, ZONE_DEV)
        return pltpu.make_async_remote_copy(
            src_ref=part.at[rows, :],
            dst_ref=from_next if side == 0 else from_prev,
            send_sem=part_send.at[side],
            recv_sem=part_recv.at[side],
            device_id=device,
            device_id_type=MESH,
        )

    for side in range(2):

        @pl.when(sides[side][0])
        def _(side=side):
            hand_over(side).start()

    grad[...] = part[ZONE_DEV : 2 * ZONE_DEV, :]

    for side, buffer in ((0, from_next), (1, from_prev)):

        @pl.when(sides[1 - side][0])
        def _(side=side, buffer=buffer):
            hand_over(side).wait_recv()
            grad[...] += buffer[...]

    for c in range(n_chunk):
        for q in range(GROUPS):
            own_back(c, q).wait()
            for d in range(1, n_harm):
                back(d, c, q).wait()
        for d in range(1, n_harm):
            arrive(d, c).wait_send()
    for side in range(2):

        @pl.when(sides[side][0])
        def _(side=side):
            hand_over(side).wait_send()
            for c in range(n_chunk):
                for d in range(n_harm):
                    halo(d, c, side).wait_send()


def body(
    n_harm,
    n_node,
    adjoint,
    source,
    rad_coeff,
    capacity,
    inv_diag,
    blocks,
    block_cols,
    zone_of,
    heater_weight,
):
    rows, _, nodes = adjoint.shape
    n_chunk = rows // ROWS
    harmonics = n_harm * rows
    order = np.arange(harmonics).reshape(n_harm, n_chunk, ROWS).transpose(1, 0, 2).reshape(-1)
    basis = fourier_basis(harmonics)
    half = harmonics // 2
    rate_k = np.where(order < half, order, -(order - half)).astype(np.float32)[:, None]
    rate_k = np.broadcast_to(rate_k, (harmonics, WIDTH))

    row_blocks = nodes // 128
    sent = adjoint.reshape(n_chunk, ROWS, n_harm, row_blocks, 128).transpose(2, 0, 3, 1, 4)
    vmem = pl.BlockSpec(memory_space=pltpu.VMEM)
    smem = pl.BlockSpec(memory_space=pltpu.SMEM)
    hbm = pl.BlockSpec(memory_space=pl.ANY)
    piece = (n_harm, n_chunk, ROWS, nodes)
    dma = pltpu.SemaphoreType.DMA
    returned, gradient = pl.pallas_call(
        functools.partial(kernel, n_harm, n_node, n_chunk),
        out_shape=(
            jax.ShapeDtypeStruct(piece, jnp.bfloat16),
            jax.ShapeDtypeStruct((ZONE_DEV, harmonics), jnp.float32),
        ),
        in_specs=[vmem, hbm, hbm, hbm, vmem, vmem, vmem, vmem, smem, vmem, vmem, vmem],
        out_specs=(vmem, vmem),
        scratch_shapes=[pltpu.VMEM((n_harm, 3 * row_blocks, ROWS, 128), jnp.bfloat16)] * n_chunk
        + [
            pltpu.VMEM(piece, jnp.float32),
            pltpu.VMEM(rad_coeff.shape, jnp.bfloat16),
            pltpu.VMEM(blocks.shape, jnp.bfloat16),
            pltpu.VMEM(piece, jnp.bfloat16),
            pltpu.VMEM((256, nodes), jnp.bfloat16),
            pltpu.VMEM((128, harmonics), jnp.float32),
            pltpu.VMEM((ZONE_DEV, harmonics), jnp.float32),
            pltpu.VMEM((ZONE_DEV, harmonics), jnp.float32),
            dma((3 + n_chunk,)),
            dma((n_harm, n_chunk)),
            dma((n_harm, n_chunk)),
            dma((2, n_harm, n_chunk)),
            dma((2, n_harm, n_chunk)),
            dma((n_harm, n_chunk, GROUPS)),
            dma((n_harm, n_chunk, GROUPS)),
            dma((n_chunk, GROUPS)),
            dma((2,)),
            dma((2,)),
        ],
        compiler_params=pltpu.CompilerParams(
            collective_id=0, has_side_effects=True, vmem_limit_bytes=48 * 2**20
        ),
    )(
        sent,
        source.reshape(piece),
        rad_coeff,
        blocks,
        capacity[None, :],
        inv_diag[None, :],
        heater_weight[None, :],
        zone_of[None, :],
        block_cols.T,
        jnp.asarray(basis[:, order]),
        jnp.asarray(basis.T[order]),
        jnp.asarray(rate_k),
    )
    return returned.reshape(n_harm, rows, nodes).transpose(1, 0, 2), gradient


def solution(mesh):
    in_specs = (
        P("harm", None, "node"),
        P(None, ("harm", "node")),
        P(None, ("harm", "node")),
        P(("harm", "node")),
        P(("harm", "node")),
        P(("harm", "node"), None, None, None),
        P(("harm", "node"), None),
        P(("harm", "node")),
        P(("harm", "node")),
    )
    out_specs = (P("harm", None, "node"), P(("harm", "node"), None))
    step = functools.partial(body, mesh.shape["harm"], mesh.shape["node"])
    return jax.shard_map(step, mesh=mesh, in_specs=in_specs, out_specs=out_specs, check_vma=False)
```

time: 117 us -> 73.7 us (0.63)
  the two profiles are of different devices: /device:TPU:4 before, /device:TPU:0 now
where the time goes in v1:
time: 73.7 us; the launch traced here: 73.6 us
  Pallas kernels  65.3 us (89%)
  local copies, waits for them, and re-layouts  7.5 us (10%)
  between operations  0.81 us (1%)
    pallas_call x1, Pallas kernels, body(): pl.pallas_call(functools.partial(kernel, n_harm, n_node, n_chunk), out_sh...  65.3 us
    reshape x2, local copies, waits for them, and re-layouts, body(): adjoint.reshape(n_chunk, ROWS, n_harm, row_blocks, 128)  4.99 us
    reshape x1, local copies, waits for them, and re-layouts, body(): return (returned.reshape(n_harm, rows, nodes).transpose(1, 0, 2), gradient)  1.78 us

profile of v1, /device:TPU:0, one launch (start us, length us, event | category | flops | bytes accessed | tf_op | source)
XLA Modules:
  0.0 73.6 jit_solution(7721104046250517967)
XLA Ops:
  0.6 0.0 copy-start.2
  0.6 0.0 copy-start.3
  0.7 0.0 copy-start.9
  0.7 0.0 copy-start.6
  0.7 0.0 copy-start.7
  0.7 0.0 copy-start.8
  0.7 0.0 copy-start.5
  0.7 0.0 copy-start.4
  0.7 0.0 copy-start.1
  0.7 0.0 copy-start
  0.7 3.1 %reshape.16 = bf16[2,16,4,32,128]{4,3,2,1,0:T(8,128)(2,1)} reshape(bf16[32,4,4096]{2,1,0:T(4,128)(2,1)} %param.12) | data formatting | bytes 2097152 | tf_op jit(solution)/shard_map/reshape | solution.py:347
  3.8 1.9 %copy.22 = bf16[2,16,4,32,128]{4,1,3,0,2:T(8,128)(2,1)S(1)} copy(bf16[2,16,4,32,128]{4,3,2,1,0:T(8,128)(2,1)} %reshape.16) | data formatting | bytes 2097152 | tf_op jit(solution)/shard_map/reshape | solution.py:347
  5.7 0.0 copy-done.9
  5.7 0.1 jit_solution_.3.rate_k
  5.8 0.0 copy-done.2
  5.8 0.0 copy-done.3
  5.8 0.0 copy-done.6
  5.9 0.0 copy-done.7
  5.9 0.0 copy-done.8
  5.9 0.0 copy-done.5
  5.9 0.0 copy-done.4
  5.9 0.0 copy-done.1
  5.9 0.0 copy-done
  5.9 65.3 %shard_map.131 = (bf16[4,2,16,4096]{3,2,1,0:T(8,128)(2,1)S(1)}, f32[40,128]{1,0:T(8,128)S(1)}) custom-call(bf16[4,2,32,16,128]{4,3,2,1,0:T(8,128)(2,1)S(1)} %bitcast.13, f32[4,2,16,4096]{3,2,1,0:T(8,128)S(1)} %bitcast.14, bf16[128,4096]{1,0:T(8,128)(2,1)S(1)} %copy-done.1, bf16[32,4,128,128]{3,2,1,0:T(8,128)(2,1)} %blk_any.1, f32[1,4096]{1,0:T(1,128)S(1)} %bitcast.16, ...), custom_call_target="tpu_custom_call" | custom-call | tf_op jit(solution)/shard_map/pallas_call | solution.py:353
  71.2 1.8 %copy.23 = bf16[4,32,4096]{2,0,1:T(4,128)(2,1)} copy(bf16[4,32,4096]{2,1,0:T(8,128)(2,1)S(1)} %bitcast.15) | data formatting | bytes 2097152 | tf_op jit(solution)/shard_map/reshape | solution.py:399
  73.0 0.6 copy.25
Async XLA Ops:
  0.6 5.2 %copy-start.2 = (bf16[128,128]{1,0:T(8,128)(2,1)S(1)}, bf16[128,128]{1,0:T(8,128)(2,1)}, u32[]{:S(2)}) copy-start(bf16[128,128]{1,0:T(8,128)(2,1)} %constant.7.clone.fourier_t) | copy-start | bytes 98308
  0.6 5.2 %copy-start.3 = (bf16[128,128]{1,0:T(8,128)(2,1)S(1)}, bf16[128,128]{1,0:T(8,128)(2,1)}, u32[]{:S(2)}) copy-start(bf16[128,128]{1,0:T(8,128)(2,1)} %constant.6.clone.fourier) | copy-start | bytes 98308
  0.7 5.1 %copy-start.9 = (f32[128]{0:T(128)S(1)}, f32[128]{0:T(128)}, u32[]{:S(2)}) copy-start(f32[128]{0:T(128)} %constant.8.clone) | copy-start | bytes 1540
  0.7 5.2 %copy-start.6 = (f32[4096]{0:T(1024)S(1)}, f32[4096]{0:T(1024)}, u32[]{:S(2)}) copy-start(f32[4096]{0:T(1024)} %param.20) | copy-start | bytes 49156
  0.7 5.2 %copy-start.7 = (s32[4096]{0:T(1024)S(1)}, s32[4096]{0:T(1024)}, u32[]{:S(2)}) copy-start(s32[4096]{0:T(1024)} %param.19) | copy-start | bytes 49156
  0.7 5.2 %copy-start.8 = (s32[32,4]{0,1:T(4,128)S(1)}, s32[32,4]{0,1:T(4,128)}, u32[]{:S(2)}) copy-start(s32[32,4]{0,1:T(4,128)} %param.18) | copy-start | bytes 1540
  0.7 5.2 %copy-start.5 = (f32[4096]{0:T(1024)S(1)}, f32[4096]{0:T(1024)}, u32[]{:S(2)}) copy-start(f32[4096]{0:T(1024)} %param.16) | copy-start | bytes 49156
  0.7 5.2 %copy-start.4 = (f32[4096]{0:T(1024)S(1)}, f32[4096]{0:T(1024)}, u32[]{:S(2)}) copy-start(f32[4096]{0:T(1024)} %param.15) | copy-start | bytes 49156
  0.7 5.2 %copy-start.1 = (bf16[128,4096]{1,0:T(8,128)(2,1)S(1)}, bf16[128,4096]{1,0:T(8,128)(2,1)}, u32[]{:S(2)}) copy-start(bf16[128,4096]{1,0:T(8,128)(2,1)} %rad_any.1) | copy-start | bytes 3145732
  0.7 5.2 %copy-start = (f32[128,4096]{1,0:T(8,128)S(1)}, f32[128,4096]{1,0:T(8,128)}, u32[]{:S(2)}) copy-start(f32[128,4096]{1,0:T(8,128)} %param.13) | copy-start | bytes 6291460

commit v2 on v1

--- a/solution.py
+++ b/solution.py
@@ -11,8 +11,9 @@
 
 ZONE_DEV = 40
 ROWS = 16
+UNROLL = 4
 GROUPS = 4
-WIDTH = 256
+WIDTH = 512
 MESH = pl.DeviceIdType.MESH
 NT = (((1,), (1,)), ((), ()))
 
@@ -38,7 +39,7 @@
     n_harm,
     n_node,
     n_chunk,
-    adj,
+    given,
     src_any,
     rad_any,
     blk_any,
@@ -56,6 +57,7 @@
 ):
     ext = scratch[:n_chunk]
     (
+        adj,
         src,
         rad,
         blk,
@@ -75,8 +77,8 @@
         part_send,
         part_recv,
     ) = scratch[n_chunk:]
-    row_blocks = adj.shape[2]
-    nodes = row_blocks * 128
+    nodes = given.shape[2]
+    row_blocks = nodes // 128
     chunk_rows = n_harm * ROWS
     me_h = lax.axis_index("harm")
     me_n = lax.axis_index("node")
@@ -150,13 +152,20 @@
             def _(side=side):
                 halo(d, c, side).start()
 
+    def split(h, c):
+        for i in range(row_blocks):
+            adj[h, c, i] = given[h, c * ROWS : (c + 1) * ROWS, i * 128 : (i + 1) * 128]
+
     for c in range(n_chunk):
         for d in range(1, n_harm):
+            split(lax.rem(me_h + d, n_harm), c)
             arrive(d, c).start()
+        split(me_h, c)
         own[c].start()
         start_halo(0, c)
-    for load in loads:
-        load.start()
+        if c == 0:
+            for load in loads:
+                load.start()
 
     zone_row = lax.broadcasted_iota(jnp.int32, (128, WIDTH), 0)
 
@@ -171,18 +180,88 @@
 
     lax.fori_loop(0, nodes // WIDTH, select_step, 0)
 
+    def block_of(c, index):
+        return jnp.concatenate([ext[c][h, index] for h in range(n_harm)], axis=0)
+
+    group = nodes // GROUPS
+    half = chunk_rows // 2
+
+    def back(d, c, q):
+        peer = lax.rem(me_h + d, n_harm)
+        return pltpu.make_async_remote_copy(
+            src_ref=upd.at[peer, c, :, pl.ds(q * group, group)],
+            dst_ref=ret.at[me_h, c, :, pl.ds(q * group, group)],
+            send_sem=out_send.at[d, c, q],
+            recv_sem=out_recv.at[d, c, q],
+            device_id=(peer, me_n),
+            device_id_type=MESH,
+        )
+
+    def own_back(c, q):
+        return pltpu.make_async_copy(
+            upd.at[me_h, c, :, pl.ds(q * group, group)],
+            ret.at[me_h, c, :, pl.ds(q * group, group)],
+            own_sem.at[c, q],
+        )
+
+    def start_back(c, q):
+        for d in range(1, n_harm):
+            back(d, c, q).start()
+        own_back(c, q).start()
+
+    def wait_halo(c):
+        for side in range(2):
+
+            @pl.when(sides[1 - side][0])
+            def _(side=side):
+                for d in range(n_harm):
+                    halo(d, c, side).wait_recv()
+
+    def conduct(c, start, finish):
+        results = []
+        for u in range(UNROLL):
+            b = start + u
+            at = pl.ds(pl.multiple_of(b * 128, 128), 128)
+            lam = block_of(c, row_blocks + b)
+            taken = [lam]
+            for s in range(1, blk.shape[1]):
+                col = cols[s, b] - (pos - 1) * row_blocks
+                col = jnp.minimum(jnp.maximum(col, 0), 3 * row_blocks - 1)
+                taken.append(block_of(c, col))
+            conduction = lax.dot_general(
+                jnp.concatenate(taken, axis=1),
+                jnp.concatenate([blk[b, s] for s in range(blk.shape[1])], axis=1),
+                NT,
+                preferred_element_type=jnp.float32,
+            )
+            residual = src[:, c, :, at].reshape(chunk_rows, 128) - conduction
+            if finish:
+                residual = lam.astype(jnp.float32) + inv_diag[:, at] * residual
+            results.append((at, residual))
+        for at, result in results:
+            result = result.reshape(n_harm, ROWS, 128)
+            if finish:
+                upd[:, c, :, at] = result.astype(jnp.bfloat16)
+            else:
+                src[:, c, :, at] = result
+
+    last_chunk = n_chunk - 1
     for c in range(n_chunk):
         own[c].wait()
         for d in range(1, n_harm):
             arrive(d, c).wait_recv()
             start_halo(d, c)
-    for load in loads:
-        load.wait()
-
-    def block_of(c, index):
-        return jnp.concatenate([ext[c][h, index] for h in range(n_harm)], axis=0)
-
-    half = chunk_rows // 2
+        if c == 0:
+            for load in loads:
+                load.wait()
+        if c < last_chunk:
+            wait_halo(c)
+
+            def conduct_step(i, carry, c=c):
+                conduct(c, i * UNROLL, False)
+                return carry
+
+            lax.fori_loop(0, row_blocks // UNROLL, conduct_step, 0)
 
     def local_step(i, carry):
         at = pl.ds(pl.multiple_of(i * WIDTH, WIDTH), WIDTH)
@@ -202,69 +281,29 @@
             rows = slice(c * chunk_rows, (c + 1) * chunk_rows)
             rate = rate_k[rows, :] * swapped
             rest = src[:, c, :, at].reshape(chunk_rows, WIDTH) - (cap * rate + radiative[rows])
-            src[:, c, :, at] = rest.reshape(n_harm, ROWS, WIDTH)
+            if c < last_chunk:
+                new = lam + inv_diag[:, at] * rest
+                upd[:, c, :, at] = new.astype(jnp.bfloat16).reshape(n_harm, ROWS, WIDTH)
+            else:
+                src[:, c, :, at] = rest.reshape(n_harm, ROWS, WIDTH)
         return carry
 
-    lax.fori_loop(0, nodes // WIDTH, local_step, 0)
-
-    group = nodes // GROUPS
-    group_blocks = group // 128
-
-    def back(d, c, q):
-        peer = lax.rem(me_h + d, n_harm)
-        return pltpu.make_async_remote_copy(
-            src_ref=upd.at[peer, c, :, pl.ds(q * group, group)],
-            dst_ref=ret.at[me_h, c, :, pl.ds(q * group, group)],
-            send_sem=out_send.at[d, c, q],
-            recv_sem=out_recv.at[d, c, q],
-            device_id=(peer, me_n),
-            device_id_type=MESH,
-        )
-
-    def own_back(c, q):
-        return pltpu.make_async_copy(
-            upd.at[me_h, c, :, pl.ds(q * group, group)],
-            ret.at[me_h, c, :, pl.ds(q * group, group)],
-            own_sem.at[c, q],
-        )
-
-    for c in range(n_chunk):
-        for side in range(2):
-
-            @pl.when(sides[1 - side][0])
-            def _(side=side, c=c):
-                for d in range(n_harm):
-                    halo(d, c, side).wait_recv()
-
-        for q in range(GROUPS):
-
-            def block_step(i, carry, c=c, q=q):
-                b = q * group_blocks + i
-                at = pl.ds(pl.multiple_of(b * 128, 128), 128)
-                lam = block_of(c, row_blocks + b)
-                taken = [lam]
-                for s in range(1, blk.shape[1]):
-                    col = cols[s, b] - (pos - 1) * row_blocks
-                    col = jnp.minimum(jnp.maximum(col, 0), 3 * row_blocks - 1)
-                    taken.append(block_of(c, col))
-                conductance = jnp.concatenate(
-                    [blk[b, s] for s in range(blk.shape[1])], axis=1
-                )
-                conduction = lax.dot_general(
-                    jnp.concatenate(taken, axis=1),
-                    conductance,
-                    NT,
-                    preferred_element_type=jnp.float32,
-                )
-                residual = src[:, c, :, at].reshape(chunk_rows, 128) - conduction
-                new = lam.astype(jnp.float32) + inv_diag[:, at] * residual
-                upd[:, c, :, at] = new.astype(jnp.bfloat16).reshape(n_harm, ROWS, 128)
-                return carry
-
-            lax.fori_loop(0, group_blocks, block_step, 0, unroll=2)
-            for d in range(1, n_harm):
-                back(d, c, q).start()
-            own_back(c, q).start()
+    steps = group // WIDTH
+    for q in range(GROUPS):
+        lax.fori_loop(q * steps, (q + 1) * steps, local_step, 0)
+        for c in range(last_chunk):
+            start_back(c, q)
+
+    wait_halo(last_chunk)
+    group_steps = group // 128 // UNROLL
+    for q in range(GROUPS):
+
+        def final_step(i, carry):
+            conduct(last_chunk, i * UNROLL, True)
+            return carry
+
+        lax.fori_loop(q * group_steps, (q + 1) * group_steps, final_step, 0)
+        start_back(last_chunk, q)
 
     part[...] = jnp.zeros_like(part)
 
@@ -344,7 +383,7 @@
     rate_k = np.broadcast_to(rate_k, (harmonics, WIDTH))
 
     row_blocks = nodes // 128
-    sent = adjoint.reshape(n_chunk, ROWS, n_harm, row_blocks, 128).transpose(2, 0, 3, 1, 4)
+    sent = adjoint.transpose(1, 0, 2)
     vmem = pl.BlockSpec(memory_space=pltpu.VMEM)
     smem = pl.BlockSpec(memory_space=pltpu.SMEM)
     hbm = pl.BlockSpec(memory_space=pl.ANY)
@@ -360,6 +399,7 @@
         out_specs=(vmem, vmem),
         scratch_shapes=[pltpu.VMEM((n_harm, 3 * row_blocks, ROWS, 128), jnp.bfloat16)] * n_chunk
         + [
+            pltpu.VMEM((n_harm, n_chunk, row_blocks, ROWS, 128), jnp.bfloat16),
             pltpu.VMEM(piece, jnp.float32),
             pltpu.VMEM(rad_coeff.shape, jnp.bfloat16),
             pltpu.VMEM(blocks.shape, jnp.bfloat16),

time: 73.7 us -> 82.5 us (1.12)
  local copies, waits for them, and re-layouts: 7.5 us -> 12.8 us
  Pallas kernels: 65.3 us -> 68.4 us
    unnamed x21 -> x20, local copies, waits for them, and re-layouts: 0.66 us -> 10.3 us
    reshape x2 -> x0, local copies, waits for them, and re-layouts: 4.99 us -> none  [body(): adjoint.reshape(n_chunk, ROWS, n_harm, row_blocks, 128)]
    pallas_call x1, Pallas kernels: 65.3 us -> 68.4 us  [body(): pl.pallas_call(functools.partial(kernel, n_harm, n_node, n_chunk), out_sh...]
where the time goes in v2:
time: 82.5 us; the launch traced here: 81.9 us
  Pallas kernels  68.4 us (83%)
  local copies, waits for them, and re-layouts  12.8 us (16%)
    pallas_call x1, Pallas kernels, body(): pl.pallas_call(functools.partial(kernel, n_harm, n_node, n_chunk), out_sh...  68.4 us
    unnamed x20, local copies, waits for them, and re-layouts  10.3 us
    reshape x1, local copies, waits for them, and re-layouts, body(): return (returned.reshape(n_harm, rows, nodes).transpose(1, 0, 2), gradient)  1.78 us

profile of v2, /device:TPU:0, one launch (start us, length us, event | category | flops | bytes accessed | tf_op | source)
XLA Modules:
  0.0 81.9 jit_solution(1675957447762331867)
XLA Ops:
  0.6 1.8 %copy.19 = bf16[32,4,4096]{2,0,1:T(8,128)(2,1)S(1)} copy(bf16[32,4,4096]{2,1,0:T(4,128)(2,1)} %param.12) | data formatting | bytes 2097152 | tf_op args[0]
  2.4 0.7 jit_solution_.3.rate_k
  3.2 0.0 copy-start
  3.2 1.6 %copy-done = f32[128,4096]{1,0:T(8,128)S(1)} copy-done((f32[128,4096]{1,0:T(8,128)S(1)}, f32[128,4096]{1,0:T(8,128)}, u32[]{:S(2)}) %copy-start) | copy-done | bytes 2097176
  4.8 0.0 copy-start.1
  4.8 1.2 %copy-done.1 = bf16[128,4096]{1,0:T(8,128)(2,1)S(1)} copy-done((bf16[128,4096]{1,0:T(8,128)(2,1)S(1)}, bf16[128,4096]{1,0:T(8,128)(2,1)}, u32[]{:S(2)}) %copy-start.1) | copy-done | bytes 1048600
  6.0 0.0 copy-start.2
  6.0 0.8 copy-done.2
  6.8 0.0 copy-start.3
  6.8 0.8 copy-done.3
  7.5 0.0 copy-start.4
  7.5 0.7 copy-done.4
  8.2 0.0 copy-start.5
  8.2 0.7 copy-done.5
  9.0 0.0 copy-start.6
  9.0 0.7 copy-done.6
  9.7 0.0 copy-start.7
  9.7 0.7 copy-done.7
  10.4 0.0 copy-start.8
  10.4 0.7 copy-done.8
  11.1 68.4 %shard_map.131 = (bf16[4,2,16,4096]{3,2,1,0:T(8,128)(2,1)S(1)}, f32[40,128]{1,0:T(8,128)S(1)}) custom-call(bf16[4,32,4096]{2,1,0:T(8,128)(2,1)S(1)} %bitcast.13, f32[4,2,16,4096]{3,2,1,0:T(8,128)S(1)} %bitcast.14, bf16[128,4096]{1,0:T(8,128)(2,1)S(1)} %copy-done.1, bf16[32,4,128,128]{3,2,1,0:T(8,128)(2,1)} %blk_any.1, f32[1,4096]{1,0:T(1,128)S(1)} %bitcast.16, ...), custom_call_target="tpu_custom_call" | custom-call | tf_op jit(solution)/shard_map/pallas_call | solution.py:392
  79.5 1.8 %copy.18 = bf16[4,32,4096]{2,0,1:T(4,128)(2,1)} copy(bf16[4,32,4096]{2,1,0:T(8,128)(2,1)S(1)} %bitcast.15) | data formatting | bytes 2097152 | tf_op jit(solution)/shard_map/reshape | solution.py:439
  81.3 0.6 copy.21
Async XLA Ops:
  3.2 1.6 %copy-start = (f32[128,4096]{1,0:T(8,128)S(1)}, f32[128,4096]{1,0:T(8,128)}, u32[]{:S(2)}) copy-start(f32[128,4096]{1,0:T(8,128)} %param.13) | copy-start | bytes 6291460
  4.8 1.2 %copy-start.1 = (bf16[128,4096]{1,0:T(8,128)(2,1)S(1)}, bf16[128,4096]{1,0:T(8,128)(2,1)}, u32[]{:S(2)}) copy-start(bf16[128,4096]{1,0:T(8,128)(2,1)} %rad_any.1) | copy-start | bytes 3145732
  6.0 0.8 copy-start.2
  6.8 0.8 copy-start.3
  7.5 0.7 copy-start.4
  8.2 0.7 copy-start.5
  9.0 0.7 copy-start.6
  9.7 0.7 copy-start.7
  10.4 0.7 copy-start.8

commit v3 on v2

--- a/solution.py
+++ b/solution.py
@@ -43,20 +43,25 @@
     src_any,
     rad_any,
     blk_any,
-    capacity,
-    inv_diag,
-    weight,
-    zone,
+    cap_any,
+    inv_any,
+    weight_any,
+    zone_any,
     cols,
-    fourier,
-    fourier_t,
-    rate_k,
+    fourier_any,
+    fourier_t_any,
     ret,
     grad,
     *scratch,
 ):
     ext = scratch[:n_chunk]
     (
+        capacity,
+        inv_diag,
+        weight,
+        zone,
+        fourier,
+        fourier_t,
         adj,
         src,
         rad,
@@ -76,6 +81,7 @@
         own_sem,
         part_send,
         part_recv,
+        small_sem,
     ) = scratch[n_chunk:]
     nodes = given.shape[2]
     row_blocks = nodes // 128
@@ -104,6 +110,22 @@
         for c in range(n_chunk)
     ]
 
+    small = [
+        pltpu.make_async_copy(source, target, small_sem.at[i])
+        for i, (source, target) in enumerate(
+            (
+                (zone_any, zone),
+                (weight_any, weight),
+                (cap_any, capacity),
+                (inv_any, inv_diag),
+                (fourier_any, fourier),
+                (fourier_t_any, fourier_t),
+            )
+        )
+    ]
+    for load in small:
+        load.start()
+
     barrier = pltpu.get_barrier_semaphore()
     for d in range(1, n_harm):
         peer = lax.rem(me_h + d, n_harm)
@@ -166,6 +188,9 @@
         if c == 0:
             for load in loads:
                 load.start()
+
+    for load in small:
+        load.wait()
 
     zone_row = lax.broadcasted_iota(jnp.int32, (128, WIDTH), 0)
 
@@ -263,6 +288,13 @@
 
             lax.fori_loop(0, row_blocks // UNROLL, conduct_step, 0)
 
+    row = lax.broadcasted_iota(jnp.int32, (chunk_rows, WIDTH), 0)
+    rate_k = []
+    for c in range(n_chunk):
+        natural = (row // ROWS) * (n_chunk * ROWS) + c * ROWS + row % ROWS
+        middle = n_chunk * n_harm * ROWS // 2
+        rate_k.append(jnp.where(natural < middle, natural, middle - natural).astype(jnp.float32))
+
     def local_step(i, carry):
         at = pl.ds(pl.multiple_of(i * WIDTH, WIDTH), WIDTH)
         first = row_blocks + i * (WIDTH // 128)
@@ -279,7 +311,7 @@
             lam = pieces[c].astype(jnp.float32)
             swapped = jnp.concatenate([lam[half:], lam[:half]], axis=0)
             rows = slice(c * chunk_rows, (c + 1) * chunk_rows)
-            rate = rate_k[rows, :] * swapped
+            rate = rate_k[c] * swapped
             rest = src[:, c, :, at].reshape(chunk_rows, WIDTH) - (cap * rate + radiative[rows])
             if c < last_chunk:
                 new = lam + inv_diag[:, at] * rest
@@ -378,9 +410,6 @@
     harmonics = n_harm * rows
     order = np.arange(harmonics).reshape(n_harm, n_chunk, ROWS).transpose(1, 0, 2).reshape(-1)
     basis = fourier_basis(harmonics)
-    half = harmonics // 2
-    rate_k = np.where(order < half, order, -(order - half)).astype(np.float32)[:, None]
-    rate_k = np.broadcast_to(rate_k, (harmonics, WIDTH))
 
     row_blocks = nodes // 128
     sent = adjoint.transpose(1, 0, 2)
@@ -395,10 +424,16 @@
             jax.ShapeDtypeStruct(piece, jnp.bfloat16),
             jax.ShapeDtypeStruct((ZONE_DEV, harmonics), jnp.float32),
         ),
-        in_specs=[vmem, hbm, hbm, hbm, vmem, vmem, vmem, vmem, smem, vmem, vmem, vmem],
+        in_specs=[vmem] + [hbm] * 7 + [smem, hbm, hbm],
         out_specs=(vmem, vmem),
         scratch_shapes=[pltpu.VMEM((n_harm, 3 * row_blocks, ROWS, 128), jnp.bfloat16)] * n_chunk
         + [
+            pltpu.VMEM((1, nodes), jnp.float32),
+            pltpu.VMEM((1, nodes), jnp.float32),
+            pltpu.VMEM((1, nodes), jnp.float32),
+            pltpu.VMEM((1, nodes), jnp.int32),
+            pltpu.VMEM((harmonics, harmonics), jnp.bfloat16),
+            pltpu.VMEM((harmonics, harmonics), jnp.bfloat16),
             pltpu.VMEM((n_harm, n_chunk, row_blocks, ROWS, 128), jnp.bfloat16),
             pltpu.VMEM(piece, jnp.float32),
             pltpu.VMEM(rad_coeff.shape, jnp.bfloat16),
@@ -418,6 +453,7 @@
             dma((n_chunk, GROUPS)),
             dma((2,)),
             dma((2,)),
+            dma((6,)),
         ],
         compiler_params=pltpu.CompilerParams(
             collective_id=0, has_side_effects=True, vmem_limit_bytes=48 * 2**20
@@ -434,7 +470,6 @@
         block_cols.T,
         jnp.asarray(basis[:, order]),
         jnp.asarray(basis.T[order]),
-        jnp.asarray(rate_k),
     )
     return returned.reshape(n_harm, rows, nodes).transpose(1, 0, 2), gradient
 

time: 82.5 us -> 82 us (level)
  no operation moved by 1% of the time
where the time goes in v3:
time: 82 us; the launch traced here: 81.4 us
  Pallas kernels  68.6 us (84%)
  local copies, waits for them, and re-layouts  12.1 us (15%)
    pallas_call x1, Pallas kernels, body(): pl.pallas_call(functools.partial(kernel, n_harm, n_node, n_chunk), out_sh...  68.6 us
    unnamed x20, local copies, waits for them, and re-layouts  10.3 us
    reshape x1, local copies, waits for them, and re-layouts, body(): return (returned.reshape(n_harm, rows, nodes).transpose(1, 0, 2), gradient)  1.78 us

profile of v3, /device:TPU:0, one launch (start us, length us, event | category | flops | bytes accessed | tf_op | source)
XLA Modules:
  0.0 81.4 jit_solution(9670536085271286014)
XLA Ops:
  0.6 1.8 %copy.18 = bf16[32,4,4096]{2,0,1:T(8,128)(2,1)S(1)} copy(bf16[32,4,4096]{2,1,0:T(4,128)(2,1)} %param.11) | data formatting | bytes 2097152 | tf_op args[0]
  2.4 0.0 copy-start
  2.4 1.6 %copy-done = f32[128,4096]{1,0:T(8,128)S(1)} copy-done((f32[128,4096]{1,0:T(8,128)S(1)}, f32[128,4096]{1,0:T(8,128)}, u32[]{:S(2)}) %copy-start) | copy-done | bytes 2097176
  4.0 0.0 copy-start.1
  4.0 1.2 %copy-done.1 = bf16[128,4096]{1,0:T(8,128)(2,1)S(1)} copy-done((bf16[128,4096]{1,0:T(8,128)(2,1)S(1)}, bf16[128,4096]{1,0:T(8,128)(2,1)}, u32[]{:S(2)}) %copy-start.1) | copy-done | bytes 1048600
  5.3 0.0 copy-start.2
  5.3 0.8 copy-done.2
  6.0 0.0 copy-start.3
  6.0 0.8 copy-done.3
  6.8 0.0 copy-start.4
  6.8 0.7 copy-done.4
  7.5 0.0 copy-start.5
  7.5 0.7 copy-done.5
  8.2 0.0 copy-start.6
  8.2 0.7 copy-done.6
  8.9 0.0 copy-start.7
  8.9 0.7 copy-done.7
  9.6 0.0 copy-start.8
  9.6 0.7 copy-done.8
  10.3 68.6 %shard_map.122 = (bf16[4,2,16,4096]{3,2,1,0:T(8,128)(2,1)S(1)}, f32[40,128]{1,0:T(8,128)S(1)}) custom-call(bf16[4,32,4096]{2,1,0:T(8,128)(2,1)S(1)} %bitcast.13, f32[4,2,16,4096]{3,2,1,0:T(8,128)S(1)} %bitcast.14, bf16[128,4096]{1,0:T(8,128)(2,1)S(1)} %copy-done.1, bf16[32,4,128,128]{3,2,1,0:T(8,128)(2,1)} %blk_any.1, f32[1,4096]{1,0:T(1,128)S(1)} %bitcast.16, ...), custom_call_target="tpu_custom_call" | custom-call | tf_op jit(solution)/shard_map/pallas_call | solution.py:421
  79.0 1.8 %copy.17 = bf16[4,32,4096]{2,0,1:T(4,128)(2,1)} copy(bf16[4,32,4096]{2,1,0:T(8,128)(2,1)S(1)} %bitcast.15) | data formatting | bytes 2097152 | tf_op jit(solution)/shard_map/reshape | solution.py:474
  80.8 0.6 copy.20
Async XLA Ops:
  2.4 1.6 %copy-start = (f32[128,4096]{1,0:T(8,128)S(1)}, f32[128,4096]{1,0:T(8,128)}, u32[]{:S(2)}) copy-start(f32[128,4096]{1,0:T(8,128)} %param.12) | copy-start | bytes 6291460
  4.0 1.2 %copy-start.1 = (bf16[128,4096]{1,0:T(8,128)(2,1)S(1)}, bf16[128,4096]{1,0:T(8,128)(2,1)}, u32[]{:S(2)}) copy-start(bf16[128,4096]{1,0:T(8,128)(2,1)} %rad_any.1) | copy-start | bytes 3145732
  5.3 0.8 copy-start.2
  6.0 0.8 copy-start.3
  6.8 0.7 copy-start.4
  7.5 0.7 copy-start.5
  8.2 0.7 copy-start.6
  8.9 0.7 copy-start.7
  9.6 0.7 copy-start.8

commit v4 on v3

--- a/solution.py
+++ b/solution.py
@@ -242,7 +242,7 @@
                 for d in range(n_harm):
                     halo(d, c, side).wait_recv()
 
-    def conduct(c, start, finish):
+    def conduct(c, start):
         results = []
         for u in range(UNROLL):
             b = start + u
@@ -260,17 +260,10 @@
                 preferred_element_type=jnp.float32,
             )
             residual = src[:, c, :, at].reshape(chunk_rows, 128) - conduction
-            if finish:
-                residual = lam.astype(jnp.float32) + inv_diag[:, at] * residual
-            results.append((at, residual))
+            results.append((at, lam.astype(jnp.float32) + inv_diag[:, at] * residual))
         for at, result in results:
-            result = result.reshape(n_harm, ROWS, 128)
-            if finish:
-                upd[:, c, :, at] = result.astype(jnp.bfloat16)
-            else:
-                src[:, c, :, at] = result
-
-    last_chunk = n_chunk - 1
+            upd[:, c, :, at] = result.reshape(n_harm, ROWS, 128).astype(jnp.bfloat16)
+
     for c in range(n_chunk):
         own[c].wait()
         for d in range(1, n_harm):
@@ -279,14 +272,6 @@
         if c == 0:
             for load in loads:
                 load.wait()
-        if c < last_chunk:
-            wait_halo(c)
-
-            def conduct_step(i, carry, c=c):
-                conduct(c, i * UNROLL, False)
-                return carry
-
-            lax.fori_loop(0, row_blocks // UNROLL, conduct_step, 0)
 
     row = lax.broadcasted_iota(jnp.int32, (chunk_rows, WIDTH), 0)
     rate_k = []
@@ -313,29 +298,22 @@
             rows = slice(c * chunk_rows, (c + 1) * chunk_rows)
             rate = rate_k[c] * swapped
             rest = src[:, c, :, at].reshape(chunk_rows, WIDTH) - (cap * rate + radiative[rows])
-            if c < last_chunk:
-                new = lam + inv_diag[:, at] * rest
-                upd[:, c, :, at] = new.astype(jnp.bfloat16).reshape(n_harm, ROWS, WIDTH)
-            else:
-                src[:, c, :, at] = rest.reshape(n_harm, ROWS, WIDTH)
+            src[:, c, :, at] = rest.reshape(n_harm, ROWS, WIDTH)
         return carry
 
-    steps = group // WIDTH
-    for q in range(GROUPS):
-        lax.fori_loop(q * steps, (q + 1) * steps, local_step, 0)
-        for c in range(last_chunk):
+    lax.fori_loop(0, nodes // WIDTH, local_step, 0)
+
+    group_steps = group // 128 // UNROLL
+    for c in range(n_chunk):
+        wait_halo(c)
+        for q in range(GROUPS):
+
+            def final_step(i, carry, c=c):
+                conduct(c, i * UNROLL)
+                return carry
+
+            lax.fori_loop(q * group_steps, (q + 1) * group_steps, final_step, 0)
             start_back(c, q)
-
-    wait_halo(last_chunk)
-    group_steps = group // 128 // UNROLL
-    for q in range(GROUPS):
-
-        def final_step(i, carry):
-            conduct(last_chunk, i * UNROLL, True)
-            return carry
-
-        lax.fori_loop(q * group_steps, (q + 1) * group_steps, final_step, 0)
-        start_back(last_chunk, q)
 
     part[...] = jnp.zeros_like(part)
 
@@ -415,7 +393,7 @@
     sent = adjoint.transpose(1, 0, 2)
     vmem = pl.BlockSpec(memory_space=pltpu.VMEM)
     smem = pl.BlockSpec(memory_space=pltpu.SMEM)
-    hbm = pl.BlockSpec(memory_space=pl.ANY)
+    hbm = pl.BlockSpec(memory_space=pltpu.HBM)
     piece = (n_harm, n_chunk, ROWS, nodes)
     dma = pltpu.SemaphoreType.DMA
     returned, gradient = pl.pallas_call(

time: 82 us -> 79.9 us (0.974)
  Pallas kernels: 68.6 us -> 66.6 us
    pallas_call x1, Pallas kernels: 68.6 us -> 66.6 us  [body(): pl.pallas_call(functools.partial(kernel, n_harm, n_node, n_chunk), out_sh...]
where the time goes in v4:
time: 79.9 us; the launch traced here: 79.3 us
  Pallas kernels  66.6 us (83%)
  local copies, waits for them, and re-layouts  12.1 us (15%)
    pallas_call x1, Pallas kernels, body(): pl.pallas_call(functools.partial(kernel, n_harm, n_node, n_chunk), out_sh...  66.6 us
    unnamed x20, local copies, waits for them, and re-layouts  10.3 us
    reshape x1, local copies, waits for them, and re-layouts, body(): return (returned.reshape(n_harm, rows, nodes).transpose(1, 0, 2), gradient)  1.78 us

profile of v4, /device:TPU:0, one launch (start us, length us, event | category | flops | bytes accessed | tf_op | source)
XLA Modules:
  0.0 79.3 jit_solution(11568654453690129679)
XLA Ops:
  0.6 1.8 %copy.18 = bf16[32,4,4096]{2,0,1:T(8,128)(2,1)S(1)} copy(bf16[32,4,4096]{2,1,0:T(4,128)(2,1)} %param.11) | data formatting | bytes 2097152 | tf_op args[0]
  2.4 0.0 copy-start
  2.4 1.6 %copy-done = f32[128,4096]{1,0:T(8,128)S(1)} copy-done((f32[128,4096]{1,0:T(8,128)S(1)}, f32[128,4096]{1,0:T(8,128)}, u32[]{:S(2)}) %copy-start) | copy-done | bytes 2097176
  4.0 0.0 copy-start.1
  4.0 1.2 %copy-done.1 = bf16[128,4096]{1,0:T(8,128)(2,1)S(1)} copy-done((bf16[128,4096]{1,0:T(8,128)(2,1)S(1)}, bf16[128,4096]{1,0:T(8,128)(2,1)}, u32[]{:S(2)}) %copy-start.1) | copy-done | bytes 1048600
  5.3 0.0 copy-start.2
  5.3 0.8 copy-done.2
  6.0 0.0 copy-start.3
  6.0 0.8 copy-done.3
  6.8 0.0 copy-start.4
  6.8 0.7 copy-done.4
  7.5 0.0 copy-start.5
  7.5 0.7 copy-done.5
  8.2 0.0 copy-start.6
  8.2 0.7 copy-done.6
  8.9 0.0 copy-start.7
  8.9 0.7 copy-done.7
  9.6 0.0 copy-start.8
  9.6 0.7 copy-done.8
  10.3 66.6 %shard_map.122 = (bf16[4,2,16,4096]{3,2,1,0:T(8,128)(2,1)S(1)}, f32[40,128]{1,0:T(8,128)S(1)}) custom-call(bf16[4,32,4096]{2,1,0:T(8,128)(2,1)S(1)} %bitcast.13, f32[4,2,16,4096]{3,2,1,0:T(8,128)S(1)} %bitcast.14, bf16[128,4096]{1,0:T(8,128)(2,1)S(1)} %copy-done.1, bf16[32,4,128,128]{3,2,1,0:T(8,128)(2,1)} %blk_any.1, f32[1,4096]{1,0:T(1,128)S(1)} %bitcast.16, ...), custom_call_target="tpu_custom_call" | custom-call | tf_op jit(solution)/shard_map/pallas_call | solution.py:399
  76.9 1.8 %copy.17 = bf16[4,32,4096]{2,0,1:T(4,128)(2,1)} copy(bf16[4,32,4096]{2,1,0:T(8,128)(2,1)S(1)} %bitcast.15) | data formatting | bytes 2097152 | tf_op jit(solution)/shard_map/reshape | solution.py:452
  78.7 0.6 copy.20
Async XLA Ops:
  2.4 1.6 %copy-start = (f32[128,4096]{1,0:T(8,128)S(1)}, f32[128,4096]{1,0:T(8,128)}, u32[]{:S(2)}) copy-start(f32[128,4096]{1,0:T(8,128)} %param.12) | copy-start | bytes 6291460
  4.0 1.2 %copy-start.1 = (bf16[128,4096]{1,0:T(8,128)(2,1)S(1)}, bf16[128,4096]{1,0:T(8,128)(2,1)}, u32[]{:S(2)}) copy-start(bf16[128,4096]{1,0:T(8,128)(2,1)} %rad_any.1) | copy-start | bytes 3145732
  5.3 0.8 copy-start.2
  6.0 0.8 copy-start.3
  6.8 0.7 copy-start.4
  7.5 0.7 copy-start.5
  8.2 0.7 copy-start.6
  8.9 0.7 copy-start.7
  9.6 0.7 copy-start.8
